TPU v7x, 128 devices: a whole 4x4x4 slice. The times are simulated.
128 devices in a mesh: row: 8 (over y, core), col: 16 (over z, x).
Axes of the slice: x: 4, y: 4, z: 4, core: 2. Of those that a mesh axis runs over, the one named last changes fastest.
Arguments:
- pair_count: int32 [2], replicated, may hold values from 2304 to 4608, as said below
- coupling: bfloat16 [2, 4608, 4608], P(None, 'row', 'col'), may hold values from -6 to 6
- amplitudes: bfloat16 [2, 4608, 4608], P(None, 'row', 'col'), may hold values from -0.09375 to 0.09375
- integrals: bfloat16 [2, 4608, 4608], P(None, 'row', 'col'), may hold values from -6 to 6
Outputs:
- cycle_term: bfloat16 [2, 4608, 4608], P(None, 'row', 'col')
Inputs may be any that keep to these rules, and one draw needn't show every extreme that they name: `pair_count`: one of the two blocks has exactly 4608 live pairs.
All inputs are finite; a program needn't handle non-finite values.
Results may differ from a plain program's by a relative error of at most 0.0049.
Values may be sent and summed in bfloat16 or wider, within the bound.
A program may use at most 128 MiB of HBM per device.

v0:
```python
import jax
import jax.numpy as jnp
from jax import lax
from jax.sharding import PartitionSpec as P


def cycle_blocks(amps, coup, ints):
    wide_amps = lax.all_gather(amps, "col", axis=2, tiled=True)
    left = wide_amps
    inter = jnp.einsum(
        "gik,gkj->gij",
        left,
        lax.all_gather(ints, "row", axis=1, tiled=True),
        preferred_element_type=jnp.float32,
    )
    mixed = (coup.astype(jnp.float32) + 0.5 * inter).astype(jnp.bfloat16)
    wide_mixed = lax.all_gather(mixed, "col", axis=2, tiled=True)
    left = wide_mixed
    result = jnp.einsum(
        "gik,gkj->gij",
        left,
        lax.all_gather(amps, "row", axis=1, tiled=True),
        preferred_element_type=jnp.float32,
    )
    return result.astype(jnp.bfloat16)


def per_device(pair_count, coupling, amplitudes, integrals):
    rows_local = coupling.shape[1]
    cols_local = coupling.shape[2]
    row_first = lax.axis_index("row") * rows_local
    col_first = lax.axis_index("col") * cols_local
    row_ids = row_first + jnp.arange(rows_local, dtype=jnp.int32)
    col_ids = col_first + jnp.arange(cols_local, dtype=jnp.int32)
    row_live = row_ids[None, :] < pair_count[:, None]
    col_live = col_ids[None, :] < pair_count[:, None]
    mask = (row_live[:, :, None] & col_live[:, None, :]).astype(jnp.bfloat16)
    amps = amplitudes * mask
    coup = coupling * mask
    ints = integrals * mask
    pieces = []
    for block in range(coupling.shape[0]):
        pieces.append(
            cycle_blocks(amps[block : block + 1], coup[block : block + 1], ints[block : block + 1])
        )
    return jnp.concatenate(pieces, axis=0)


def solution(mesh):
    in_specs = (P(), P(None, "row", "col"), P(None, "row", "col"), P(None, "row", "col"))
    out_specs = P(None, "row", "col")
    return jax.shard_map(
        per_device, mesh=mesh, in_specs=in_specs, out_specs=out_specs, check_vma=False
    )
```

profile of v0, /device:TPU:1, one launch (start us, length us, event | category | flops | bytes accessed | tf_op | source)
XLA Modules:
  0.0 456.1 jit_solution(14824971063095576185)
XLA Ops:
  6.5 0.7 broadcast_compare_fusion
  7.3 0.7 broadcast_compare_fusion.1
  8.0 2.1 and_select_fusion.2
  10.1 0.1 fusion.72
  10.2 2.0 copy.9
  12.2 0.0 all-gather.9.cloned.1.call-start
  12.2 0.9 fusion.73
  13.2 0.0 all-gather.19.cloned.1.call-start
  13.2 2.0 copy.13
  15.4 0.5 all-gather.17.cloned.1.call-update
  15.9 2.9 copy.11
  18.9 0.0 all-gather.23.cloned.1.call-start
  18.9 2.9 copy.15
  21.8 0.0 all-gather.13.cloned.1.call-start
  21.9 38.3 %all-gather.11.cloned.1.call-done = bf16[1,4608,288]{2,0,1:T(2,128)(2,1)} async-done(((bf16[1,576,288]{2,0,1:T(2,128)(2,1)}), bf16[1,4608,288]{2,0,1:T(2,128)(2,1)}) %all-gather.11.cloned.1.call-update) | async-done | bytes 2654224 | tf_op jit(solution)/shard_map/all_gather | solution.py:13
  60.2 16.5 %copy.10 = bf16[1,4608,288]{1,2,0:T(8,128)(2,1)S(1)} copy(bf16[1,4608,288]{2,0,1:T(2,128)(2,1)} %all-gather.11.cloned.1.call-done) | data formatting | bytes 5308416 | tf_op jit(solution)/shard_map/all_gather | solution.py:13
  76.7 44.9 %all-gather.9.cloned.1.call-done = bf16[1,576,4608]{1,2,0:T(8,128)(2,1)} async-done(((bf16[1,576,288]{1,2,0:T(8,128)(2,1)}), bf16[1,576,4608]{1,2,0:T(8,128)(2,1)}) %all-gather.9.cloned.1.call-update) | async-done | bytes 5308432 | tf_op jit(solution)/shard_map/all_gather | solution.py:8
  121.6 5.6 %fusion.42 = bf16[1,576,288]{1,2,0:T(8,128)(2,1)} fusion(bf16[1,576,4608]{1,2,0:T(8,128)(2,1)} %all-gather.9.cloned.1.call-done, bf16[1,4608,288]{1,2,0:T(8,128)(2,1)S(1)} %copy.10, bf16[2,576,288]{1,2,0:T(8,128)(2,1)S(1)} %get-tuple-element.9), kind=kOutput, calls=%fused_computation.21 | convolution fusion | flops 1529487360 | bytes 8626176 | tf_op jit(solution)/shard_map/gik,gkj->gij/dot_general | solution.py:10
  127.3 0.0 all-gather.21.cloned.1.call-start
  127.3 40.2 %all-gather.19.cloned.1.call-done = bf16[1,4608,288]{2,0,1:T(2,128)(2,1)} async-done(((bf16[1,576,288]{2,0,1:T(2,128)(2,1)}), bf16[1,4608,288]{2,0,1:T(2,128)(2,1)}) %all-gather.19.cloned.1.call-update) | async-done | bytes 2654224 | tf_op jit(solution)/shard_map/all_gather | solution.py:13
  167.6 16.5 %copy.14 = bf16[1,4608,288]{1,2,0:T(8,128)(2,1)S(1)} copy(bf16[1,4608,288]{2,0,1:T(2,128)(2,1)} %all-gather.19.cloned.1.call-done) | data formatting | bytes 5308416 | tf_op jit(solution)/shard_map/all_gather | solution.py:13
  184.1 44.8 %all-gather.17.cloned.1.call-done = bf16[1,576,4608]{1,2,0:T(8,128)(2,1)} async-done(((bf16[1,576,288]{1,2,0:T(8,128)(2,1)}), bf16[1,576,4608]{1,2,0:T(8,128)(2,1)}) %all-gather.17.cloned.1.call-update) | async-done | bytes 5308432 | tf_op jit(solution)/shard_map/all_gather | solution.py:8
  228.9 5.6 %fusion.47 = bf16[1,576,288]{1,2,0:T(8,128)(2,1)} fusion(bf16[1,576,4608]{1,2,0:T(8,128)(2,1)} %all-gather.17.cloned.1.call-done, bf16[1,4608,288]{1,2,0:T(8,128)(2,1)S(1)} %copy.14, bf16[2,576,288]{1,2,0:T(8,128)(2,1)S(1)} %get-tuple-element.9), kind=kOutput, calls=%fused_computation.22 | convolution fusion | flops 1529487360 | bytes 8626176 | tf_op jit(solution)/shard_map/gik,gkj->gij/dot_general | solution.py:10
  234.5 40.1 %all-gather.15.cloned.1.call-done = bf16[1,4608,288]{2,0,1:T(2,128)(2,1)} async-done(((bf16[1,576,288]{2,0,1:T(2,128)(2,1)}), bf16[1,4608,288]{2,0,1:T(2,128)(2,1)}) %all-gather.15.cloned.1.call-update) | async-done | bytes 2654224 | tf_op jit(solution)/shard_map/all_gather | solution.py:22
  274.7 15.8 %copy.12 = bf16[1,4608,288]{1,2,0:T(8,128)(2,1)} copy(bf16[1,4608,288]{2,0,1:T(2,128)(2,1)} %all-gather.15.cloned.1.call-done) | data formatting | bytes 5308416 | tf_op jit(solution)/shard_map/all_gather | solution.py:22
  290.5 30.1 %all-gather.23.cloned.1.call-done = bf16[1,4608,288]{2,0,1:T(2,128)(2,1)} async-done(((bf16[1,576,288]{2,0,1:T(2,128)(2,1)}), bf16[1,4608,288]{2,0,1:T(2,128)(2,1)}) %all-gather.23.cloned.1.call-update) | async-done | bytes 2654224 | tf_op jit(solution)/shard_map/all_gather | solution.py:22
  320.6 16.5 %copy.16 = bf16[1,4608,288]{1,2,0:T(8,128)(2,1)S(1)} copy(bf16[1,4608,288]{2,0,1:T(2,128)(2,1)} %all-gather.23.cloned.1.call-done) | data formatting | bytes 5308416 | tf_op jit(solution)/shard_map/all_gather | solution.py:22
  337.1 44.9 %all-gather.13.cloned.1.call-done = bf16[1,576,4608]{1,2,0:T(8,128)(2,1)} async-done(((bf16[1,576,288]{1,2,0:T(8,128)(2,1)}), bf16[1,576,4608]{1,2,0:T(8,128)(2,1)}) %all-gather.13.cloned.1.call-update) | async-done | bytes 5308432 | tf_op jit(solution)/shard_map/all_gather | solution.py:17
  382.0 5.7 %fusion.67 = bf16[1,576,288]{1,2,0:T(8,128)(2,1)S(1)} fusion(bf16[1,576,4608]{1,2,0:T(8,128)(2,1)} %all-gather.13.cloned.1.call-done, bf16[1,4608,288]{1,2,0:T(8,128)(2,1)} %copy.12), kind=kOutput, calls=%fused_computation.26 | convolution fusion | flops 1528989696 | bytes 8294400 | tf_op jit(solution)/shard_map/gik,gkj->gij/dot_general | solution.py:19
  387.7 55.6 %all-gather.21.cloned.1.call-done = bf16[1,576,4608]{1,2,0:T(8,128)(2,1)} async-done(((bf16[1,576,288]{1,2,0:T(8,128)(2,1)}), bf16[1,576,4608]{1,2,0:T(8,128)(2,1)}) %all-gather.21.cloned.1.call-update) | async-done | bytes 5308432 | tf_op jit(solution)/shard_map/all_gather | solution.py:17
  443.4 4.9 %fusion.62 = bf16[1,576,288]{1,2,0:T(8,128)(2,1)S(1)} fusion(bf16[1,576,4608]{1,2,0:T(8,128)(2,1)} %all-gather.21.cloned.1.call-done, bf16[1,4608,288]{1,2,0:T(8,128)(2,1)S(1)} %copy.16), kind=kOutput, calls=%fused_computation.25 | convolution fusion | flops 1528989696 | bytes 8294400 | tf_op jit(solution)/shard_map/gik,gkj->gij/dot_general | solution.py:19
  448.3 1.0 pad_maximum_fusion
  (12 shorter events, 0.2 us)
Async XLA Ops:
  6.5 53.7 %all-gather.11.cloned.1.call-start = ((), (), s32[]{:S(2)}) async-start(), calls=%async_computation.1 | async-start | bytes 7962624 | tf_op jit(solution)/shard_map/all_gather | solution.py:13
  12.2 109.5 %all-gather.9.cloned.1.call-start = ((), (), s32[]{:S(2)}) async-start(), calls=%async_computation | async-start | bytes 6266880 | tf_op jit(solution)/shard_map/all_gather | solution.py:8
  13.2 154.4 %all-gather.19.cloned.1.call-start = ((), (), s32[]{:S(2)}) async-start(), calls=%async_computation.5 | async-start | bytes 7962624 | tf_op jit(solution)/shard_map/all_gather | solution.py:13
  15.3 213.6 %all-gather.17.cloned.1.call-start = ((), (), s32[]{:S(2)}) async-start(), calls=%async_computation.4 | async-start | bytes 6266880 | tf_op jit(solution)/shard_map/all_gather | solution.py:8
  15.9 258.8 %all-gather.15.cloned.1.call-start = ((), (), s32[]{:S(2)}) async-start(), calls=%async_computation.3 | async-start | bytes 7962624 | tf_op jit(solution)/shard_map/all_gather | solution.py:22
  18.9 301.7 %all-gather.23.cloned.1.call-start = ((), (), s32[]{:S(2)}) async-start(), calls=%async_computation.7 | async-start | bytes 7962624 | tf_op jit(solution)/shard_map/all_gather | solution.py:22
  21.8 360.2 %all-gather.13.cloned.1.call-start = ((), (), s32[]{:S(2)}) async-start(), calls=%async_computation.2 | async-start | bytes 6266880 | tf_op jit(solution)/shard_map/all_gather | solution.py:17
  127.3 316.1 %all-gather.21.cloned.1.call-start = ((), (), s32[]{:S(2)}) async-start(), calls=%async_computation.6 | async-start | bytes 6266880 | tf_op jit(solution)/shard_map/all_gather | solution.py:17
Sparse Core Ops, SparseCore 0:
  12.3 47.8 all-gather.10
  62.3 59.2 all-gather.8
  123.3 44.2 all-gather.18
  169.6 59.2 all-gather.16
  230.4 44.2 all-gather.14
  276.2 44.3 all-gather.22
  322.7 59.2 all-gather.12
  384.2 59.1 all-gather.20
where the time goes:
time: 458 us; the launch traced here: 456 us
  waiting for transfers between devices  340 us (74%)
  local copies, waits for them, and re-layouts  76.1 us (17%)
  matrix products  21.8 us (5%)
  between operations  13.6 us (3%)
    all_gather x2, waiting for transfers between devices, cycle_blocks(): wide_mixed = lax.all_gather(mixed, 'col', axis=2, tiled=True)  101 us
    all_gather x2, waiting for transfers between devices, cycle_blocks(): wide_amps = lax.all_gather(amps, 'col', axis=2, tiled=True)  89.7 us
    all_gather x2, waiting for transfers between devices, cycle_blocks(): lax.all_gather(ints, 'row', axis=1, tiled=True)  78.6 us
    all_gather x2, waiting for transfers between devices, cycle_blocks(): lax.all_gather(amps, 'row', axis=1, tiled=True)  70.2 us
    all_gather x2, local copies, waits for them, and re-layouts, cycle_blocks(): lax.all_gather(ints, 'row', axis=1, tiled=True)  33 us
    all_gather x2, local copies, waits for them, and re-layouts, cycle_blocks(): lax.all_gather(amps, 'row', axis=1, tiled=True)  32.3 us
    dot_general x2, matrix products, cycle_blocks(): jnp.einsum('gik,gkj->gij', left, lax.all_gather(ints, 'row', axis=1, tile...  11.3 us
    dot_general x2, matrix products, cycle_blocks(): jnp.einsum('gik,gkj->gij', left, lax.all_gather(amps, 'row', axis=1, tile...  10.6 us
  transfers between devices with their start and end apart: 8, of which 8 were waited for; matrix products, arithmetic and copies ran while one was open for 20% of the time, Pallas kernels for 0%

commit v1 on v0

v1 whole, which is shorter than its diff:
```python
import jax
import jax.numpy as jnp
from jax import lax
from jax.experimental import pallas as pl
from jax.experimental.pallas import tpu as pltpu
from jax.sharding import PartitionSpec as P

MESH = pl.DeviceIdType.MESH
F32, BF16 = jnp.float32, jnp.bfloat16
ROWS, COLS = 576, 288
Q = 3
R = ROWS // Q
G = R // 4
PR = 2 * R + G
H = ROWS // 2
RG = 80
PV = 2 * H + RG


def swap4(parts):
    group = lax.broadcasted_iota(jnp.int32, parts[0].shape, 1) // 32
    out = []
    for b in range(4):
        total = None
        for a in range(4):
            v = parts[a] if a == b else pltpu.roll(parts[a], (32 * (a - b)) % 128, 1)
            total = v if total is None else jnp.where(group == a, v, total)
        out.append(total)
    return out


def kernel(
    count, w_hbm, t_hbm, v_hbm, out,
    w_in, t_in, v_in, load_sem,
    ts, tl, tl_s1, tl_r1, tl_s2, tl_r2, tl_sw,
    ws, wp, w_sw,
    vp, vm, vr, vx, v_as, v_ar, v_s1, v_r1, v_s2, v_r2,
    tp, tm, tr, tx, t_as, t_ar, t_s1, t_r1, t_s2, t_r2,
    mb, m_s1, m_r1, m_s2, m_r2,
    lhs1, cs1, own1, d1, d2, d_s1, d_r1, d_s2, d_r2,
    lhs2, cs2, own2, e1, e2, e_s1, e_r1, e_s2, e_r2,
    fo, ob, o_s, o_r,
):
    row, col = lax.axis_index("row"), lax.axis_index("col")
    y, c = row // 2, lax.rem(row, 2)
    z, x = col // 4, lax.rem(col, 4)

    def at(i, n):
        return lax.rem(i + n + 8, 4)

    def dev(dx=0, dy=0, dz=0, core=None):
        return (at(y, dy) * 2 + (c if core is None else core), at(z, dz) * 4 + at(x, dx))

    partner = dev(core=1 - c)
    pending = []

    def send(src, dst, ss, rs, to):
        copy = pltpu.make_async_remote_copy(src, dst, ss, rs, device_id=to, device_id_type=MESH)
        copy.start()
        pending.append(copy)

    def got(dst, rs):
        pltpu.make_async_remote_copy(dst, dst, rs, rs, device_id=partner, device_id_type=MESH).wait_recv()

    loads = [
        pltpu.make_async_copy(a, b, load_sem.at[i])
        for i, (a, b) in enumerate(((v_hbm, v_in), (t_hbm, t_in), (w_hbm, w_in)))
    ]
    for load in loads:
        load.start()
    barrier = pltpu.get_barrier_semaphore()
    friends = [dev(dx=d, core=k) for d in (1, 2, 3) for k in (0, 1)] + [partner]
    friends += [dev(dz=d, core=k) for d in (1, -1) for k in (0, 1)]
    friends += [dev(dy=d) for d in (1, -1)]
    for friend in friends:
        pl.semaphore_signal(barrier, inc=1, device_id=friend, device_id_type=MESH)

    def masked(ref, h, r0, n, c0, w):
        live = count[h]
        rid = row * ROWS + r0 + lax.broadcasted_iota(jnp.int32, (n, w), 0)
        cid = col * COLS + c0 + lax.broadcasted_iota(jnp.int32, (n, w), 1)
        return jnp.where((rid < live) & (cid < live), ref[h, r0 : r0 + n, c0 : c0 + w].astype(F32), 0.0)

    def pack_rows(ref, dst, h, q):
        r0 = q * R
        dst[h, q, 0:R] = masked(ref, h, r0, R, 0, 128).astype(BF16)
        dst[h, q, R : 2 * R] = masked(ref, h, r0, R, 128, 128).astype(BF16)
        strips = [masked(ref, h, r0 + g * G, G, 256, 32) for g in range(4)]
        dst[h, q, 2 * R : PR] = jnp.concatenate(strips, axis=1).astype(BF16)

    def pack_right(ref, dst, h, s):
        r0 = s * H
        dst[h, s, 0:H] = masked(ref, h, r0, H, 0, 128).astype(BF16)
        dst[h, s, H : 2 * H] = masked(ref, h, r0, H, 128, 128).astype(BF16)
        strips = []
        for g in range(4):
            n = min(RG, H - g * RG)
            strip = masked(ref, h, r0 + g * RG, n, 256, 32)
            if n < RG:
                strip = jnp.concatenate([strip, jnp.zeros((RG - n, 32), F32)], axis=0)
            strips.append(strip)
        dst[h, s, 2 * H : PV] = jnp.concatenate(strips, axis=1).astype(BF16)

    def exchange(vp, vm, vx, as_, ar, go):
        for s in range(2):
            tx_ = 2 * c + s
            for h in range(2):
                mine = (tx_ == x) & (c == h)
                to = (y * 2 + h, z * 4 + tx_)
                copies = (
                    (vp.at[h, s, 0 : 2 * H], vm.at[y, x], as_.at[s, h, 0], ar.at[x, 0]),
                    (vp.at[h, s, 2 * H : PV], vx.at[x], as_.at[s, h, 1], ar.at[x, 1]),
                )

                @pl.when(jnp.logical_not(mine))
                def _():
                    for a, b, ss, rs in copies:
                        r = pltpu.make_async_remote_copy(a, b, ss, rs, device_id=to, device_id_type=MESH)
                        if go:
                            r.start()
                        else:
                            r.wait_send()

                if go:

                    @pl.when(mine)
                    def _():
                        for a, b, ss, rs in copies:
                            pltpu.make_async_copy(a, b, rs).start()

    def y_send(vm, vx, vr, ar, s1, r1, o):
        if o < 4:
            xo = at(x, o)
            src = vm.at[y, xo]
            got(src, ar.at[xo, 0])
        else:
            for i in range(4):
                got(vx.at[i], ar.at[i, 1])
            for g, v in enumerate(swap4([vx[i].astype(F32) for i in range(4)])):
                n = min(RG, H - g * RG)
                vr[y, g * RG : g * RG + n] = v[:n].astype(BF16)
            src = vr.at[y]
        for d in (0, 1):
            send(src, src, s1.at[d, o], r1.at[d, o], dev(dy=1 - 2 * d))

    def y_part(vm, vr, k, o, d):
        if o < 4:
            return vm.at[k, at(x, o), pl.ds(d * H, H)]
        return vr.at[k, pl.ds(d * (H // 2), H // 2)]

    def y_all(vm, vr, k, o):
        return vm.at[k, at(x, o)] if o < 4 else vr.at[k]

    def y_forward(vm, vr, r1, s2, r2, o):
        for d in (0, 1):
            k = at(y, 2 * d - 1)
            got(y_all(vm, vr, k, o), r1.at[d, o])
            part = y_part(vm, vr, k, o, d)
            send(part, part, s2.at[d, o], r2.at[d, o], dev(dy=1 - 2 * d))

    def y_last(vm, vr, r2, o):
        for d in (0, 1):
            got(y_part(vm, vr, at(y, 2), o, d), r2.at[d, o])

    def z_forward(buf, r1, s2, r2, q):
        for d in (0, 1):
            k, p = at(z, 2 * d - 1), d * Q + q
            got(buf.at[k, p], r1.at[d, p])
            send(buf.at[k, p], buf.at[k, p], s2.at[d, q], r2.at[d, q], dev(dz=1 - 2 * d))

    def z_last(buf, r1, r2, q):
        for d in (0, 1):
            k, p = at(z, 2 * d - 1), (1 - d) * Q + q
            got(buf.at[k, p], r1.at[d, p])
            got(buf.at[at(z, 2), d * Q + q], r2.at[d, q])

    def make_left(buf, lhs, q):
        for half in (0, 1):
            p, r0 = half * Q + q, half * R
            for k in range(4):
                lhs[q, r0 : r0 + R, k * 256 : k * 256 + 128] = buf[k, p, 0:R]
                lhs[q, r0 : r0 + R, k * 256 + 128 : k * 256 + 256] = buf[k, p, R : 2 * R]
            for g, v in enumerate(swap4([buf[k, p, 2 * R : PR].astype(F32) for k in range(4)])):
                lhs[q, r0 + g * G : r0 + g * G + G, 1024:1152] = v.astype(BF16)

    def dot_main(lhs, vm, cs, own, q, o):
        t = at(x, o)
        big = [jnp.concatenate([vm[k, t, 0:256], vm[k, t, H : H + 256]], axis=1) for k in range(4)]
        small = [jnp.concatenate([vm[k, t, 256:H], vm[k, t, H + 256 : 2 * H]], axis=1) for k in range(4)]
        part = jnp.dot(lhs[q], jnp.concatenate(big + small, axis=0), preferred_element_type=F32)
        for half in (0, 1):
            p = half * Q + q
            for lane in (0, 1):
                v = part[half * R : half * R + R, lane * 128 : lane * 128 + 128]
                if o == 0:
                    own[p, lane * R : lane * R + R] = v
                else:
                    cs[o - 1, p, lane * R : lane * R + R] = v.astype(BF16)

    def dot_rest(lhs, vr, cs, own, q):
        right = jnp.concatenate([vr[k, 0:256] for k in range(4)] + [vr[k, 256:H] for k in range(4)], axis=0)
        part = jnp.dot(lhs[q], right, preferred_element_type=F32)
        for half in (0, 1):
            p = half * Q + q
            by_x = swap4([part[half * R + g * G : half * R + g * G + G] for g in range(4)])
            for o in range(4):
                t = at(x, o)
                v = jnp.where(t == 0, by_x[0], jnp.where(t == 1, by_x[1], jnp.where(t == 2, by_x[2], by_x[3])))
                if o == 0:
                    own[p, 2 * R : PR] = v
                else:
                    cs[o - 1, p, 2 * R : PR] = v.astype(BF16)

    def first_hop(cs, d1, s1, r1, q):
        for d in (0, 1):
            send(cs.at[1, d * Q + q], d1.at[d, q], s1.at[d, q], r1.at[d, q], dev(dx=1 - 2 * d))

    def alone(cs, d2, s2, r2, q, d):
        p = (1 - d) * Q + q
        send(cs.at[2 * d, p], d2.at[d, p], s2.at[d, p], r2.at[d, p], dev(dx=1 - 2 * d))

    def relay(cs, d1, d2, r1, s2, r2, q):
        for d in (0, 1):
            p = d * Q + q
            got(d1.at[d, q], r1.at[d, q])
            cs[2 * d, p] = (cs[2 * d, p].astype(F32) + d1[d, q].astype(F32)).astype(BF16)
            send(cs.at[2 * d, p], d2.at[d, p], s2.at[d, p], r2.at[d, p], dev(dx=1 - 2 * d))

    def total(own, d2, r2, p):
        for d in (0, 1):
            got(d2.at[d, p], r2.at[d, p])
        return own[p] + d2[0, p].astype(F32) + d2[1, p].astype(F32)

    def mix(q):
        for half in (0, 1):
            p = half * Q + q
            mb[z, p] = (wp[p].astype(F32) + 0.5 * total(own1, d2, d_r2, p)).astype(BF16)
            for d in (0, 1):
                send(mb.at[z, p], mb.at[z, p], m_s1.at[d, p], m_r1.at[d, p], dev(dz=1 - 2 * d))

    def unpack(v, h, q):
        r0 = q * R
        out[h, r0 : r0 + R, 0:128] = v[0:R].astype(BF16)
        out[h, r0 : r0 + R, 128:256] = v[R : 2 * R].astype(BF16)
        for g in range(4):
            strip = v[2 * R : PR]
            if g:
                strip = pltpu.roll(strip, 128 - 32 * g, 1)
            out[h, r0 + g * G : r0 + g * G + G, 256:288] = strip[:, 0:32].astype(BF16)

    def finish(q):
        for half in (0, 1):
            fo[half, q] = total(own2, e2, e_r2, half * Q + q).astype(BF16)
        send(fo.at[1 - c, q], ob.at[q], o_s.at[q], o_r.at[q], partner)
        unpack(fo[c, q].astype(F32), c, q)

    def collect(q):
        got(ob.at[q], o_r.at[q])
        unpack(ob[q].astype(F32), 1 - c, q)

    V = dict(vm=vm, vr=vr)
    T = dict(vm=tm, vr=tr)

    def yv_send(o):
        y_send(vm, vx, vr, v_ar, v_s1, v_r1, o)

    def yv_fwd(o):
        y_forward(vm, vr, v_r1, v_s2, v_r2, o)

    def yt_send(o):
        y_send(tm, tx, tr, t_ar, t_s1, t_r1, o)

    def yt_fwd(o):
        y_forward(tm, tr, t_r1, t_s2, t_r2, o)

    loads[0].wait()
    for h in range(2):
        for s in range(2):
            pack_right(v_in, vp, h, s)
    pl.semaphore_wait(barrier, len(friends))
    exchange(vp, vm, vx, v_as, v_ar, True)
    loads[1].wait()
    for q in range(Q):
        for h in range(2):
            pack_rows(t_in, ts, h, q)
            for d in (0, 1):
                send(ts.at[h, q], tl.at[z, c * Q + q], tl_s1.at[d, h, q], tl_r1.at[d, c * Q + q], dev(dz=1 - 2 * d, core=h))
        send(ts.at[1 - c, q], tl.at[z, c * Q + q], tl_sw.at[0, q], tl_sw.at[1, q], partner)
        tl[z, c * Q + q] = ts[c, q]
    yv_send(0)
    for h in range(2):
        for s in range(2):
            pack_right(t_in, tp, h, s)
    exchange(tp, tm, tx, t_as, t_ar, True)
    loads[2].wait()
    for h in range(2):
        for q in range(Q):
            pack_rows(w_in, ws, h, q)
    send(ws.at[1 - c], wp.at[pl.ds(c * Q, Q)], w_sw.at[0], w_sw.at[1], partner)
    for q in range(Q):
        wp[c * Q + q] = ws[c, q]
    yv_send(2)
    z_forward(tl, tl_r1, tl_s2, tl_r2, 0)
    yv_fwd(0)
    yv_send(4)
    yv_send(1)
    yv_send(3)
    yv_fwd(2)
    z_forward(tl, tl_r1, tl_s2, tl_r2, 1)
    yv_fwd(4)

    def left_ready(q):
        z_last(tl, tl_r1, tl_r2, q)
        got(tl.at[z, (1 - c) * Q + q], tl_sw.at[1, q])
        make_left(tl, lhs1, q)

    left_ready(0)
    y_last(vm, vr, v_r2, 2)
    y_last(vm, vr, v_r2, 4)
    dot_rest(lhs1, vr, cs1, own1, 0)
    dot_main(lhs1, vm, cs1, own1, 0, 2)
    first_hop(cs1, d1, d_s1, d_r1, 0)
    z_forward(tl, tl_r1, tl_s2, tl_r2, 2)
    yv_fwd(1)
    yv_fwd(3)
    left_ready(1)
    dot_rest(lhs1, vr, cs1, own1, 1)
    dot_main(lhs1, vm, cs1, own1, 1, 2)
    first_hop(cs1, d1, d_s1, d_r1, 1)
    y_last(vm, vr, v_r2, 1)
    dot_main(lhs1, vm, cs1, own1, 0, 1)
    alone(cs1, d2, d_s2, d_r2, 0, 0)
    y_last(vm, vr, v_r2, 3)
    dot_main(lhs1, vm, cs1, own1, 0, 3)
    alone(cs1, d2, d_s2, d_r2, 0, 1)
    relay(cs1, d1, d2, d_r1, d_s2, d_r2, 0)
    for o in (2, 4, 1, 3, 0):
        yt_send(o)
    y_last(vm, vr, v_r2, 0)
    dot_main(lhs1, vm, cs1, own1, 0, 0)
    left_ready(2)
    dot_rest(lhs1, vr, cs1, own1, 2)
    dot_main(lhs1, vm, cs1, own1, 2, 2)
    first_hop(cs1, d1, d_s1, d_r1, 2)
    for q in (1, 2):
        dot_main(lhs1, vm, cs1, own1, q, 1)
        alone(cs1, d2, d_s2, d_r2, q, 0)
        dot_main(lhs1, vm, cs1, own1, q, 3)
        alone(cs1, d2, d_s2, d_r2, q, 1)
        relay(cs1, d1, d2, d_r1, d_s2, d_r2, q)
        dot_main(lhs1, vm, cs1, own1, q, 0)
    yt_fwd(2)
    got(wp.at[pl.ds((1 - c) * Q, Q)], w_sw.at[1])
    mix(0)
    yt_fwd(4)
    mix(1)
    yt_fwd(1)
    mix(2)
    yt_fwd(3)

    def mixed_ready(q):
        z_last(mb, m_r1, m_r2, q)
        make_left(mb, lhs2, q)

    z_forward(mb, m_r1, m_s2, m_r2, 0)
    yt_fwd(0)
    z_forward(mb, m_r1, m_s2, m_r2, 1)
    mixed_ready(0)
    y_last(tm, tr, t_r2, 2)
    y_last(tm, tr, t_r2, 4)
    dot_rest(lhs2, tr, cs2, own2, 0)
    dot_main(lhs2, tm, cs2, own2, 0, 2)
    first_hop(cs2, e1, e_s1, e_r1, 0)
    y_last(tm, tr, t_r2, 1)
    dot_main(lhs2, tm, cs2, own2, 0, 1)
    alone(cs2, e2, e_s2, e_r2, 0, 0)
    y_last(tm, tr, t_r2, 3)
    dot_main(lhs2, tm, cs2, own2, 0, 3)
    alone(cs2, e2, e_s2, e_r2, 0, 1)
    z_forward(mb, m_r1, m_s2, m_r2, 2)
    y_last(tm, tr, t_r2, 0)
    for q in (1, 2):
        mixed_ready(q)
        dot_rest(lhs2, tr, cs2, own2, q)
        dot_main(lhs2, tm, cs2, own2, q, 2)
        first_hop(cs2, e1, e_s1, e_r1, q)
        relay(cs2, e1, e2, e_r1, e_s2, e_r2, q - 1)
        dot_main(lhs2, tm, cs2, own2, q, 1)
        alone(cs2, e2, e_s2, e_r2, q, 0)
        dot_main(lhs2, tm, cs2, own2, q, 3)
        alone(cs2, e2, e_s2, e_r2, q, 1)
        dot_main(lhs2, tm, cs2, own2, q - 1, 0)
        if q == 2:
            finish(0)
    relay(cs2, e1, e2, e_r1, e_s2, e_r2, 2)
    dot_main(lhs2, tm, cs2, own2, 2, 0)
    finish(1)
    collect(0)
    finish(2)
    collect(1)
    collect(2)
    exchange(vp, vm, vx, v_as, v_ar, False)
    exchange(tp, tm, tx, t_as, t_ar, False)
    for copy in pending:
        copy.wait_send()


def per_device(pair_count, coupling, amplitudes, integrals):
    dma = pltpu.SemaphoreType.DMA
    shard = coupling.shape

    def piece(*lead, dtype=BF16):
        return pltpu.VMEM((*lead, PR, 128), dtype)

    def right():
        return [
            pltpu.VMEM((2, 2, PV, 128), BF16), pltpu.VMEM((4, 4, 2 * H, 128), BF16), pltpu.VMEM((4, H, 128), BF16),
            pltpu.VMEM((4, RG, 128), BF16), dma((2, 2, 2)), dma((4, 2)),
            dma((2, 5)), dma((2, 5)), dma((2, 5)), dma((2, 5)),
        ]

    def sums():
        return [
            pltpu.VMEM((Q, 2 * R, 1152), BF16), piece(3, 2 * Q), piece(2 * Q, dtype=F32), piece(2, Q), piece(2, 2 * Q),
            dma((2, Q)), dma((2, Q)), dma((2, 2 * Q)), dma((2, 2 * Q)),
        ]

    scratch = [pltpu.VMEM(shard, BF16)] * 3 + [dma((3,))]
    scratch += [piece(2, Q), piece(4, 2 * Q), dma((2, 2, Q)), dma((2, 2 * Q)), dma((2, Q)), dma((2, Q)), dma((2, Q))]
    scratch += [piece(2, Q), piece(2 * Q), dma((2,))]
    scratch += right() + right()
    scratch += [piece(4, 2 * Q), dma((2, 2 * Q)), dma((2, 2 * Q)), dma((2, Q)), dma((2, Q))]
    scratch += sums() + sums()
    scratch += [piece(2, Q), piece(Q), dma((Q,)), dma((Q,))]
    return pl.pallas_call(
        kernel,
        out_shape=jax.ShapeDtypeStruct(shard, BF16),
        in_specs=[pl.BlockSpec(memory_space=pltpu.SMEM)] + [pl.BlockSpec(memory_space=pl.ANY)] * 3,
        out_specs=pl.BlockSpec(memory_space=pltpu.VMEM),
        scratch_shapes=scratch,
        compiler_params=pltpu.CompilerParams(collective_id=0, has_side_effects=True, vmem_limit_bytes=56 << 20),
        cost_estimate=pl.CostEstimate(flops=6115295232, bytes_accessed=2654208, transcendentals=0),
        name="cycle",
    )(pair_count, coupling, amplitudes, integrals)


def solution(mesh):
    split = P(None, "row", "col")
    return jax.shard_map(per_device, mesh=mesh, in_specs=(P(), split, split, split), out_specs=split, check_vma=False)
```

time: 458 us -> 102 us (0.22)
  waiting for transfers between devices: 340 us -> 0 us
  Pallas kernels: 0 us -> 95.3 us
  local copies, waits for them, and re-layouts: 76.1 us -> 6.87 us
  matrix products: 21.8 us -> 0 us
  between operations: 13.6 us -> 0.01 us
    all_gather x8 -> x0, waiting for transfers between devices: 339 us -> none  [the longest x2 101 us: cycle_blocks(): wide_mixed = lax.all_gather(mixed, 'col', axis=2, tiled=True)]
    pallas_call x0 -> x1, Pallas kernels: none -> 95.3 us  [per_device(): pl.pallas_call(kernel, out_shape=jax.ShapeDtypeStruct(shard, BF16), in_sp...]
    all_gather x4 -> x0, local copies, waits for them, and re-layouts: 65.3 us -> none  [the longest x2 33 us: cycle_blocks(): lax.all_gather(ints, 'row', axis=1, tiled=True)]
    dot_general x4 -> x0, matrix products: 21.8 us -> none  [the longest x2 11.3 us: cycle_blocks(): jnp.einsum('gik,gkj->gij', left, lax.all_gather(ints, 'row', axis=1, tile...]
    slice x6 -> x0, local copies, waits for them, and re-layouts: 10.8 us -> none  [the longest x3 6.73 us: per_device(): amps[block:block + 1]]
    unnamed x0 -> x7, local copies, waits for them, and re-layouts: none -> 4.74 us
  transfers between devices with their start and end apart: 8 -> 0, of which waited for: 8 -> 0; matrix products, arithmetic and copies ran while one was open for 20% -> 0% of each run, Pallas kernels for 0% -> 0%
where the time goes in v1:
time: 102 us
  Pallas kernels  95.3 us (93%)
  local copies, waits for them, and re-layouts  6.87 us (7%)
    pallas_call x1, Pallas kernels, per_device(): pl.pallas_call(kernel, out_shape=jax.ShapeDtypeStruct(shard, BF16), in_sp...  95.3 us
    unnamed x7, local copies, waits for them, and re-layouts  4.74 us
    pallas_call x1, local copies, waits for them, and re-layouts, per_device(): pl.pallas_call(kernel, out_shape=jax.ShapeDtypeStruct(shard, BF16), in_sp...  2.13 us

profile of v1, /device:TPU:1, one launch (start us, length us, event | category | flops | bytes accessed | tf_op | source)
XLA Modules:
  0.0 102.2 jit_solution(5605375185883300421)
XLA Ops:
  0.0 0.0 copy-start
  0.0 2.2 %copy.5.w_hbm = bf16[2,576,288]{2,1,0:T(8,128)(2,1)} copy(bf16[2,576,288]{1,2,0:T(8,128)(2,1)} %param.5) | data formatting | bytes 1327104 | tf_op args[1]
  2.2 0.0 copy-done
  2.2 0.0 copy-start.1
  2.2 1.3 %copy.6.t_hbm = bf16[2,576,288]{2,1,0:T(8,128)(2,1)} copy(bf16[2,576,288]{1,2,0:T(8,128)(2,1)S(1)} %copy-done) | data formatting | bytes 1327104 | tf_op args[2]
  3.5 0.0 copy-done.1
  3.5 1.2 %copy.7.v_hbm = bf16[2,576,288]{2,1,0:T(8,128)(2,1)} copy(bf16[2,576,288]{1,2,0:T(8,128)(2,1)S(1)} %copy-done.1) | data formatting | bytes 1327104 | tf_op args[3]
  4.7 95.3 %cycle.1 = bf16[2,576,288]{2,1,0:T(8,128)(2,1)} custom-call(s32[2]{0:T(128)} %count.1, bf16[2,576,288]{2,1,0:T(8,128)(2,1)} %copy.5.w_hbm, bf16[2,576,288]{2,1,0:T(8,128)(2,1)} %copy.6.t_hbm, bf16[2,576,288]{2,1,0:T(8,128)(2,1)} %copy.7.v_hbm), custom_call_target="tpu_custom_call" | custom-call | flops 6115295232 | bytes 2654208 | tf_op jit(solution)/shard_map/cycle/pallas_call | solution.py:435
  100.0 2.1 %copy.8 = bf16[2,576,288]{1,2,0:T(8,128)(2,1)} copy(bf16[2,576,288]{2,1,0:T(8,128)(2,1)} %cycle.1) | data formatting | bytes 1327104 | tf_op jit(solution)/shard_map/cycle/pallas_call | solution.py:435
Async XLA Ops:
  0.0 2.2 %copy-start = (bf16[2,576,288]{1,2,0:T(8,128)(2,1)S(1)}, bf16[2,576,288]{1,2,0:T(8,128)(2,1)}, u32[]{:S(2)}) copy-start(bf16[2,576,288]{1,2,0:T(8,128)(2,1)} %param.6) | copy-start | bytes 1990660
  2.2 1.3 %copy-start.1 = (bf16[2,576,288]{1,2,0:T(8,128)(2,1)S(1)}, bf16[2,576,288]{1,2,0:T(8,128)(2,1)}, u32[]{:S(2)}) copy-start(bf16[2,576,288]{1,2,0:T(8,128)(2,1)} %param.7) | copy-start | bytes 1990660

commit v2 on v0

v2 whole, which is shorter than its diff:
```python
from typing import Any, NamedTuple

import jax
import jax.numpy as jnp
from jax import lax
from jax.experimental import pallas as pl
from jax.experimental.pallas import tpu as pltpu
from jax.sharding import PartitionSpec as P

MESH = pl.DeviceIdType.MESH
F32, BF16 = jnp.float32, jnp.bfloat16
ROWS, COLS = 576, 288
Q = 3
R = ROWS // Q
G = R // 4
PR = 2 * R + G
H = ROWS // 2
RG = 80
PV = 2 * H + RG


def swap4(parts):
    group = lax.broadcasted_iota(jnp.int32, parts[0].shape, 1) // 32
    out = []
    for b in range(4):
        total = None
        for a in range(4):
            v = parts[a] if a == b else pltpu.roll(parts[a], (32 * (a - b)) % 128, 1)
            total = v if total is None else jnp.where(group == a, v, total)
        out.append(total)
    return out

SCHEDULE = (
    ("b",), ("p", 1), ("v", 1), ("p", 0), ("v", 0), ("pt",), ("r", 0), ("r", 1), ("t", 0), ("vs", 1), ("vs", 2),
    ("vs", 4), ("t", 1), ("lf", 0), ("vs", 3), ("t", 2), ("lf", 1), ("vf", 2), ("vf", 4), ("vf", 1), ("l", 0),
    ("l", 1), ("lf", 2), ("vf", 3), ("dr", 1, 0), ("vs", 0), ("w",), ("d", 1, 0, 2), ("dr", 1, 1), ("l", 2),
    ("d", 1, 0, 1), ("ts", 2), ("d", 1, 1, 2), ("d", 1, 0, 3), ("re", 1, 0), ("vf", 0), ("d", 1, 1, 3),
    ("d", 1, 1, 1), ("dr", 1, 2), ("d", 1, 2, 2), ("d", 1, 2, 3), ("ts", 4), ("d", 1, 2, 1), ("re", 1, 1),
    ("ts", 1), ("d", 1, 0, 0), ("mix", 0), ("ts", 3), ("re", 1, 2), ("tf", 4), ("tf", 2), ("d", 1, 1, 0),
    ("mix", 1), ("ts", 0), ("mf", 0), ("d", 1, 2, 0), ("mix", 2), ("mf", 1), ("tf", 1), ("m", 0), ("tf", 3),
    ("dr", 2, 0), ("d", 2, 0, 2), ("mf", 2), ("m", 1), ("dr", 2, 1), ("d", 2, 1, 2), ("tf", 0), ("d", 2, 0, 1),
    ("d", 2, 0, 3), ("re", 2, 0), ("m", 2), ("dr", 2, 2), ("d", 2, 2, 2), ("d", 2, 1, 1), ("d", 2, 0, 0),
    ("d", 2, 2, 3), ("d", 2, 1, 0), ("d", 2, 1, 3), ("d", 2, 2, 0), ("d", 2, 2, 1), ("re", 2, 1), ("fin", 0),
    ("re", 2, 2), ("fin", 1), ("fin", 2), ("col", 0), ("col", 1), ("col", 2),
)


def kernel(
    count, w_hbm, t_hbm, v_hbm, out,
    w_in, t_in, v_in, load_sem, live,
    w_t, t_t, v_t,
    ts, tl, tl_s1, tl_r1, tl_s2, tl_r2, tl_sw,
    ws, wp, w_sw,
    vp, vm, vr, vx, v_as, v_ar, v_s1, v_r1, v_s2, v_r2,
    tp, tm, tr, tx, t_as, t_ar, t_s1, t_r1, t_s2, t_r2,
    mb, m_s1, m_r1, m_s2, m_r2,
    lhs1, cs1, own1, d1, d2, d_s1, d_r1, d_s2, d_r2,
    lhs2, cs2, own2, e1, e2, e_s1, e_r1, e_s2, e_r2,
    fo, ob, o_t, o_s, o_r,
):
    row, col = lax.axis_index("row"), lax.axis_index("col")
    y, c = row // 2, lax.rem(row, 2)
    z, x = col // 4, lax.rem(col, 4)
    a, b = jnp.where(c == 0, z, x), jnp.where(c == 0, x, z)

    def at(i, n):
        return lax.rem(i + n + 8, 4)

    def dev(dx=0, dy=0, dz=0, core=None):
        return (at(y, dy) * 2 + (c if core is None else core), at(z, dz) * 4 + at(x, dx))

    def ring(n):
        return (row, jnp.where(c == 0, at(z, n) * 4 + x, z * 4 + at(x, n)))

    def line(n):
        return (row, jnp.where(c == 0, z * 4 + at(x, n), at(z, n) * 4 + x))

    partner = dev(core=1 - c)
    pending = []

    def remote(src, dst, ss, rs, to):
        return pltpu.make_async_remote_copy(src, dst, ss, rs, device_id=to, device_id_type=MESH)

    def send(src, dst, ss, rs, to):
        copy = remote(src, dst, ss, rs, to)
        copy.start()
        pending.append(copy)

    def got(dst, rs):
        remote(dst, dst, rs, rs, partner).wait_recv()

    loads = [
        pltpu.make_async_copy(s, d, load_sem.at[i])
        for i, (s, d) in enumerate(((v_hbm, v_in), (t_hbm, t_in), (w_hbm, w_in)))
    ]
    for load in loads:
        load.start()
    barrier = pltpu.get_barrier_semaphore()
    friends = [partner] + [dev(dx=n, core=k) for n in (1, 2, 3) for k in (0, 1)]
    friends += [dev(dz=n, core=k) for n in (1, -1) for k in (0, 1)] + [dev(dy=n) for n in (1, -1)]
    for friend in friends:
        pl.semaphore_signal(barrier, inc=1, device_id=friend, device_id_type=MESH)
    for n in range(4):
        core = y // 2

        @pl.when((c == 1) & jnp.logical_not((n == z) & (y == z) & (core == 1)))
        def _():
            source = (z * 2 + core, n * 4 + x)
            pl.semaphore_signal(barrier, inc=1, device_id=source, device_id_type=MESH)

    greetings = len(friends) + 2 - jnp.where((c == 1) & (y == z) & (y >= 2), 1, 0)
    for h in range(2):
        cid = col * COLS + lax.broadcasted_iota(jnp.int32, (COLS, ROWS), 0)
        rid = row * ROWS + lax.broadcasted_iota(jnp.int32, (COLS, ROWS), 1)
        live[h] = jnp.where((rid < count[h]) & (cid < count[h]), 1.0, 0.0).astype(BF16)

    def turn(src, dst, h):
        dst[h] = jnp.transpose(src[h] * live[h])

    def pack_rows(ref, dst, h, q):
        r0 = q * R
        dst[h, q, 0:R] = ref[h, r0 : r0 + R, 0:128]
        dst[h, q, R : 2 * R] = ref[h, r0 : r0 + R, 128:256]
        strips = [ref[h, r0 + g * G : r0 + g * G + G, 256:288].astype(F32) for g in range(4)]
        dst[h, q, 2 * R : PR] = jnp.concatenate(strips, axis=1).astype(BF16)

    def pack_right(ref, dst, h, s):
        r0 = s * H
        dst[h, s, 0:H] = ref[h, r0 : r0 + H, 0:128]
        dst[h, s, H : 2 * H] = ref[h, r0 : r0 + H, 128:256]
        strips = []
        for g in range(4):
            n = min(RG, H - g * RG)
            strip = ref[h, r0 + g * RG : r0 + g * RG + n, 256:288].astype(F32)
            if n < RG:
                strip = jnp.concatenate([strip, jnp.zeros((RG - n, 32), F32)], axis=0)
            strips.append(strip)
        dst[h, s, 2 * H : PV] = jnp.concatenate(strips, axis=1).astype(BF16)

    def either(mine, copies, to, go):
        @pl.when(jnp.logical_not(mine))
        def _():
            for copy in copies:
                if go:
                    remote(*copy, to).start()
                else:
                    remote(*copy, to).wait_send()

        if go:

            @pl.when(mine)
            def _():
                for src, dst, _, rs in copies:
                    pltpu.make_async_copy(src, dst, rs).start()

    def exchange(ops, h, go):
        for s in range(2):
            to = 2 * c + s
            k, n = (y, x) if h == 0 else (to, z)
            copies = (
                (ops.p.at[h, s, 0 : 2 * H], ops.m.at[k, n], ops.as_.at[s, h, 0], ops.ar.at[n, 0]),
                (ops.p.at[h, s, 2 * H : PV], ops.x.at[n], ops.as_.at[s, h, 1], ops.ar.at[n, 1]),
            )
            if h == 0:
                either((to == x) & (c == 0), copies, (y * 2, z * 4 + to), go)
            else:
                either((to == y) & (y == z) & (c == 1), copies, (to * 2 + 1, y * 4 + x), go)

    def y_send(ops, o):
        if o < 4:
            src = ops.m.at[y, at(b, o)]
            got(src, ops.ar.at[at(b, o), 0])
        else:
            for i in range(4):
                got(ops.x.at[i], ops.ar.at[i, 1])
            for g, v in enumerate(swap4([ops.x[i].astype(F32) for i in range(4)])):
                n = min(RG, H - g * RG)
                ops.r[y, g * RG : g * RG + n] = v[:n].astype(BF16)
            src = ops.r.at[y]
        for d in (0, 1):
            send(src, src, ops.s1.at[d, o], ops.r1.at[d, o], dev(dy=1 - 2 * d))

    def y_part(ops, k, o, d):
        if o < 4:
            return ops.m.at[k, at(b, o), pl.ds(d * H, H)]
        return ops.r.at[k, pl.ds(d * (H // 2), H // 2)]

    def y_forward(ops, o):
        for d in (0, 1):
            k = at(y, 2 * d - 1)
            got(ops.m.at[k, at(b, o)] if o < 4 else ops.r.at[k], ops.r1.at[d, o])
            part = y_part(ops, k, o, d)
            send(part, part, ops.s2.at[d, o], ops.r2.at[d, o], dev(dy=1 - 2 * d))

    def y_last(ops, o):
        for d in (0, 1):
            got(y_part(ops, at(y, 2), o, d), ops.r2.at[d, o])

    def ring_forward(buf, r1, s2, r2, q):
        for d in (0, 1):
            k, p = at(a, 2 * d - 1), d * Q + q
            got(buf.at[k, p], r1.at[d, p])
            send(buf.at[k, p], buf.at[k, p], s2.at[d, q], r2.at[d, q], ring(1 - 2 * d))

    def ring_last(buf, r1, r2, q):
        for d in (0, 1):
            k, p = at(a, 2 * d - 1), (1 - d) * Q + q
            got(buf.at[k, p], r1.at[d, p])
            got(buf.at[at(a, 2), d * Q + q], r2.at[d, q])

    def make_left(buf, lhs, q):
        for half in (0, 1):
            p, r0 = half * Q + q, half * R
            for k in range(4):
                lhs[q, r0 : r0 + R, k * 256 : k * 256 + 128] = buf[k, p, 0:R]
                lhs[q, r0 : r0 + R, k * 256 + 128 : k * 256 + 256] = buf[k, p, R : 2 * R]
            for g, v in enumerate(swap4([buf[k, p, 2 * R : PR].astype(F32) for k in range(4)])):
                lhs[q, r0 + g * G : r0 + g * G + G, 1024:1152] = v.astype(BF16)

    def dot_rest(st, q):
        vr = st.ops.r
        y_last(st.ops, 4) if q == 0 else None
        right = jnp.concatenate([vr[k, 0:256] for k in range(4)] + [vr[k, 256:H] for k in range(4)], axis=0)
        part = jnp.dot(st.lhs[q], right, preferred_element_type=F32)
        for half in (0, 1):
            p = half * Q + q
            by = swap4([part[half * R + g * G : half * R + g * G + G] for g in range(4)])
            for o in range(4):
                t = at(b, o)
                v = jnp.where(t == 0, by[0], jnp.where(t == 1, by[1], jnp.where(t == 2, by[2], by[3])))
                if o == 0:
                    st.own[p, 2 * R : PR] = v
                else:
                    st.cs[o - 1, p, 2 * R : PR] = v.astype(BF16)

    def dot_main(st, q, o):
        vm, t = st.ops.m, at(b, o)
        y_last(st.ops, o) if q == 0 else None
        big = [jnp.concatenate([vm[k, t, 0:256], vm[k, t, H : H + 256]], axis=1) for k in range(4)]
        small = [jnp.concatenate([vm[k, t, 256:H], vm[k, t, H + 256 : 2 * H]], axis=1) for k in range(4)]
        part = jnp.dot(st.lhs[q], jnp.concatenate(big + small, axis=0), preferred_element_type=F32)
        for half in (0, 1):
            p = half * Q + q
            for lane in (0, 1):
                v = part[half * R : half * R + R, lane * 128 : lane * 128 + 128]
                if o == 0:
                    st.own[p, lane * R : lane * R + R] = v
                else:
                    st.cs[o - 1, p, lane * R : lane * R + R] = v.astype(BF16)
        if o == 2:
            for d in (0, 1):
                send(st.cs.at[1, d * Q + q], st.l1.at[d, q], st.s1.at[d, q], st.r1.at[d, q], line(1 - 2 * d))
        elif o:
            d = o // 2
            p = (1 - d) * Q + q
            send(st.cs.at[2 * d, p], st.l2.at[d, p], st.s2.at[d, p], st.r2.at[d, p], line(1 - 2 * d))

    def relay(st, q):
        for d in (0, 1):
            p = d * Q + q
            got(st.l1.at[d, q], st.r1.at[d, q])
            st.cs[2 * d, p] = (st.cs[2 * d, p].astype(F32) + st.l1[d, q].astype(F32)).astype(BF16)
            send(st.cs.at[2 * d, p], st.l2.at[d, p], st.s2.at[d, p], st.r2.at[d, p], line(1 - 2 * d))

    def total(st, p):
        for d in (0, 1):
            got(st.l2.at[d, p], st.r2.at[d, p])
        return st.own[p] + st.l2[0, p].astype(F32) + st.l2[1, p].astype(F32)

    def unpack(v, h, q):
        r0 = q * R
        o_t[h, r0 : r0 + R, 0:128] = v[0:R].astype(BF16)
        o_t[h, r0 : r0 + R, 128:256] = v[R : 2 * R].astype(BF16)
        for g in range(4):
            strip = v[2 * R : PR]
            if g:
                strip = pltpu.roll(strip, 128 - 32 * g, 1)
            o_t[h, r0 + g * G : r0 + g * G + G, 256:288] = strip[:, 0:32].astype(BF16)

    def turn_back(h, q):
        if q == 1:
            out[h, :, 0:384] = jnp.transpose(o_t[h, 0:384])
        if q == 2:
            out[h, :, 384:576] = jnp.transpose(o_t[h, 384:576])

    v_ops = Ops(vp, vm, vr, vx, v_as, v_ar, v_s1, v_r1, v_s2, v_r2)
    t_ops = Ops(tp, tm, tr, tx, t_as, t_ar, t_s1, t_r1, t_s2, t_r2)
    stages = {
        1: Stage(v_ops, lhs1, cs1, own1, d1, d2, d_s1, d_r1, d_s2, d_r2),
        2: Stage(t_ops, lhs2, cs2, own2, e1, e2, e_s1, e_r1, e_s2, e_r2),
    }

    def step_p(h):
        if h == 1:
            loads[0].wait()
        turn(v_in, v_t, h)
        for s in range(2):
            pack_right(v_t, vp, h, s)

    def step_b():
        pl.semaphore_wait(barrier, greetings)

    def step_v(h):
        exchange(v_ops, h, True)

    def step_pt():
        loads[1].wait()
        for h in range(2):
            turn(t_in, t_t, h)
            for q in range(Q):
                pack_rows(t_t, ts, h, q)
        for q in range(Q):
            tl[a, c * Q + q] = ts[c, q]

    def step_t(q):
        for h in range(2):
            for d in (0, 1):
                to = dev(dz=1 - 2 * d, core=0) if h == 0 else dev(dx=1 - 2 * d, core=1)
                place = z if h == 0 else x
                send(ts.at[h, q], tl.at[place, c * Q + q], tl_s1.at[d, h, q], tl_r1.at[d, c * Q + q], to)
        send(ts.at[1 - c, q], tl.at[b, c * Q + q], tl_sw.at[0, q], tl_sw.at[1, q], partner)

    def step_r(h):
        for s in range(2):
            pack_right(t_t, tp, h, s)
        exchange(t_ops, h, True)

    def step_w():
        loads[2].wait()
        for h in range(2):
            turn(w_in, w_t, h)
            for q in range(Q):
                pack_rows(w_t, ws, h, q)
        send(ws.at[1 - c], wp.at[pl.ds(c * Q, Q)], w_sw.at[0], w_sw.at[1], partner)
        for q in range(Q):
            wp[c * Q + q] = ws[c, q]

    def step_left(q):
        ring_last(tl, tl_r1, tl_r2, q)
        got(tl.at[a, (1 - c) * Q + q], tl_sw.at[1, q])
        make_left(tl, lhs1, q)

    def step_mix(q):
        if q == 0:
            got(wp.at[pl.ds((1 - c) * Q, Q)], w_sw.at[1])
        for half in (0, 1):
            p = half * Q + q
            mb[a, p] = (wp[p].astype(F32) + 0.5 * total(stages[1], p)).astype(BF16)
            for d in (0, 1):
                send(mb.at[a, p], mb.at[a, p], m_s1.at[d, p], m_r1.at[d, p], ring(1 - 2 * d))

    def step_mixed(q):
        ring_last(mb, m_r1, m_r2, q)
        make_left(mb, lhs2, q)

    def step_finish(q):
        for half in (0, 1):
            fo[half, q] = total(stages[2], half * Q + q).astype(BF16)
        send(fo.at[1 - c, q], ob.at[q], o_s.at[q], o_r.at[q], partner)
        unpack(fo[c, q].astype(F32), c, q)
        turn_back(c, q)

    def step_collect(q):
        got(ob.at[q], o_r.at[q])
        unpack(ob[q].astype(F32), 1 - c, q)
        turn_back(1 - c, q)

    steps = {
        "v": step_v, "t": step_t, "r": step_r, "w": step_w,
        "p": step_p, "b": step_b, "pt": step_pt,
        "vs": lambda o: y_send(v_ops, o), "vf": lambda o: y_forward(v_ops, o),
        "ts": lambda o: y_send(t_ops, o), "tf": lambda o: y_forward(t_ops, o),
        "lf": lambda q: ring_forward(tl, tl_r1, tl_s2, tl_r2, q), "l": step_left,
        "mf": lambda q: ring_forward(mb, m_r1, m_s2, m_r2, q), "m": step_mixed,
        "dr": lambda s, q: dot_rest(stages[s], q), "d": lambda s, q, o: dot_main(stages[s], q, o),
        "re": lambda s, q: relay(stages[s], q), "mix": step_mix,
        "fin": step_finish, "col": step_collect,
    }
    for step in SCHEDULE:
        steps[step[0]](*step[1:])
    for ops in (v_ops, t_ops):
        for h in (0, 1):
            exchange(ops, h, False)
    for copy in pending:
        copy.wait_send()


class Ops(NamedTuple):
    p: Any
    m: Any
    r: Any
    x: Any
    as_: Any
    ar: Any
    s1: Any
    r1: Any
    s2: Any
    r2: Any


class Stage(NamedTuple):
    ops: Any
    lhs: Any
    cs: Any
    own: Any
    l1: Any
    l2: Any
    s1: Any
    r1: Any
    s2: Any
    r2: Any


def per_device(pair_count, coupling, amplitudes, integrals):
    dma = pltpu.SemaphoreType.DMA
    coupling, amplitudes, integrals = (jnp.transpose(v, (0, 2, 1)) for v in (coupling, amplitudes, integrals))
    turned, shard = (2, COLS, ROWS), (2, ROWS, COLS)

    def piece(*lead, dtype=BF16):
        return pltpu.VMEM((*lead, PR, 128), dtype)

    def right():
        return [
            pltpu.VMEM((2, 2, PV, 128), BF16), pltpu.VMEM((4, 4, 2 * H, 128), BF16), pltpu.VMEM((4, H, 128), BF16),
            pltpu.VMEM((4, RG, 128), BF16), dma((2, 2, 2)), dma((4, 2)),
            dma((2, 5)), dma((2, 5)), dma((2, 5)), dma((2, 5)),
        ]

    def sums():
        return [
            pltpu.VMEM((Q, 2 * R, 1152), BF16), piece(3, 2 * Q), piece(2 * Q, dtype=F32), piece(2, Q), piece(2, 2 * Q),
            dma((2, Q)), dma((2, Q)), dma((2, 2 * Q)), dma((2, 2 * Q)),
        ]

    scratch = [pltpu.VMEM(turned, BF16)] * 3 + [dma((3,)), pltpu.VMEM(turned, BF16)] + [pltpu.VMEM(shard, BF16)] * 3
    scratch += [piece(2, Q), piece(4, 2 * Q), dma((2, 2, Q)), dma((2, 2 * Q)), dma((2, Q)), dma((2, Q)), dma((2, Q))]
    scratch += [piece(2, Q), piece(2 * Q), dma((2,))]
    scratch += right() + right()
    scratch += [piece(4, 2 * Q), dma((2, 2 * Q)), dma((2, 2 * Q)), dma((2, Q)), dma((2, Q))]
    scratch += sums() + sums()
    scratch += [piece(2, Q), piece(Q), pltpu.VMEM(shard, BF16), dma((Q,)), dma((Q,))]
    result = pl.pallas_call(
        kernel,
        out_shape=jax.ShapeDtypeStruct(turned, BF16),
        in_specs=[pl.BlockSpec(memory_space=pltpu.SMEM)] + [pl.BlockSpec(memory_space=pl.ANY)] * 3,
        out_specs=pl.BlockSpec(memory_space=pltpu.VMEM),
        scratch_shapes=scratch,
        compiler_params=pltpu.CompilerParams(collective_id=0, has_side_effects=True, vmem_limit_bytes=56 << 20),
        cost_estimate=pl.CostEstimate(flops=6115295232, bytes_accessed=2654208, transcendentals=0),
        name="cycle",
    )(pair_count, coupling, amplitudes, integrals)
    return jnp.transpose(result, (0, 2, 1))


def solution(mesh):
    split = P(None, "row", "col")
    return jax.shard_map(per_device, mesh=mesh, in_specs=(P(), split, split, split), out_specs=split, check_vma=False)
```

time: 458 us -> 87.4 us (0.19)
  waiting for transfers between devices: 340 us -> 0 us
  Pallas kernels: 0 us -> 85.2 us
  local copies, waits for them, and re-layouts: 76.1 us -> 2.04 us
  matrix products: 21.8 us -> 0 us
  between operations: 13.6 us -> 0.01 us
    all_gather x8 -> x0, waiting for transfers between devices: 339 us -> none  [the longest x2 101 us: cycle_blocks(): wide_mixed = lax.all_gather(mixed, 'col', axis=2, tiled=True)]
    pallas_call x0 -> x1, Pallas kernels: none -> 85.2 us  [per_device(): pl.pallas_call(kernel, out_shape=jax.ShapeDtypeStruct(turned, BF16), in_s...]
    all_gather x4 -> x0, local copies, waits for them, and re-layouts: 65.3 us -> none  [the longest x2 33 us: cycle_blocks(): lax.all_gather(ints, 'row', axis=1, tiled=True)]
    dot_general x4 -> x0, matrix products: 21.8 us -> none  [the longest x2 11.3 us: cycle_blocks(): jnp.einsum('gik,gkj->gij', left, lax.all_gather(ints, 'row', axis=1, tile...]
    slice x6 -> x0, local copies, waits for them, and re-layouts: 10.8 us -> none  [the longest x3 6.73 us: per_device(): amps[block:block + 1]]
  transfers between devices with their start and end apart: 8 -> 0, of which waited for: 8 -> 0; matrix products, arithmetic and copies ran while one was open for 20% -> 0% of each run, Pallas kernels for 0% -> 0%
where the time goes in v2:
time: 87.4 us; the launch traced here: 87.3 us
  Pallas kernels  85.2 us (97%)
  local copies, waits for them, and re-layouts  2.04 us (2%)
    pallas_call x1, Pallas kernels, per_device(): pl.pallas_call(kernel, out_shape=jax.ShapeDtypeStruct(turned, BF16), in_s...  85.2 us
    unnamed x1, local copies, waits for them, and re-layouts  2.04 us

profile of v2, /device:TPU:1, one launch (start us, length us, event | category | flops | bytes accessed | tf_op | source)
XLA Modules:
  0.0 87.3 jit_solution(9429069506074133966)
XLA Ops:
  0.0 85.2 %cycle.1 = bf16[2,288,576]{2,1,0:T(8,128)(2,1)} custom-call(s32[2]{0:T(128)} %count.1, bf16[2,288,576]{2,1,0:T(8,128)(2,1)} %bitcast.5, bf16[2,288,576]{2,1,0:T(8,128)(2,1)} %bitcast.6, bf16[2,288,576]{2,1,0:T(8,128)(2,1)} %bitcast.7), custom_call_target="tpu_custom_call" | custom-call | flops 6115295232 | bytes 2654208 | tf_op jit(solution)/shard_map/cycle/pallas_call | solution.py:442
  85.2 2.0 %copy.6 = bf16[2,576,288]{1,2,0:T(8,128)(2,1)} copy(bf16[2,576,288]{1,2,0:T(8,128)(2,1)} %bitcast.4) | data formatting | bytes 1327104

commit v3 on v2

--- a/solution.py
+++ b/solution.py
@@ -31,17 +31,17 @@
     return out
 
 SCHEDULE = (
-    ("b",), ("p", 1), ("v", 1), ("p", 0), ("v", 0), ("pt",), ("r", 0), ("r", 1), ("t", 0), ("vs", 1), ("vs", 2),
-    ("vs", 4), ("t", 1), ("lf", 0), ("vs", 3), ("t", 2), ("lf", 1), ("vf", 2), ("vf", 4), ("vf", 1), ("l", 0),
-    ("l", 1), ("lf", 2), ("vf", 3), ("dr", 1, 0), ("vs", 0), ("w",), ("d", 1, 0, 2), ("dr", 1, 1), ("l", 2),
-    ("d", 1, 0, 1), ("ts", 2), ("d", 1, 1, 2), ("d", 1, 0, 3), ("re", 1, 0), ("vf", 0), ("d", 1, 1, 3),
-    ("d", 1, 1, 1), ("dr", 1, 2), ("d", 1, 2, 2), ("d", 1, 2, 3), ("ts", 4), ("d", 1, 2, 1), ("re", 1, 1),
-    ("ts", 1), ("d", 1, 0, 0), ("mix", 0), ("ts", 3), ("re", 1, 2), ("tf", 4), ("tf", 2), ("d", 1, 1, 0),
-    ("mix", 1), ("ts", 0), ("mf", 0), ("d", 1, 2, 0), ("mix", 2), ("mf", 1), ("tf", 1), ("m", 0), ("tf", 3),
-    ("dr", 2, 0), ("d", 2, 0, 2), ("mf", 2), ("m", 1), ("dr", 2, 1), ("d", 2, 1, 2), ("tf", 0), ("d", 2, 0, 1),
-    ("d", 2, 0, 3), ("re", 2, 0), ("m", 2), ("dr", 2, 2), ("d", 2, 2, 2), ("d", 2, 1, 1), ("d", 2, 0, 0),
-    ("d", 2, 2, 3), ("d", 2, 1, 0), ("d", 2, 1, 3), ("d", 2, 2, 0), ("d", 2, 2, 1), ("re", 2, 1), ("fin", 0),
-    ("re", 2, 2), ("fin", 1), ("fin", 2), ("col", 0), ("col", 1), ("col", 2),
+    ("p", 1), ("b",), ("v", 1), ("p", 0), ("v", 0), ("pt",), ("r", 1), ("vs", 2), ("t", 0), ("vs", 1), ("vs", 4),
+    ("t", 1), ("t", 2), ("lf", 0), ("vs", 3), ("lf", 2), ("vf", 4), ("w",), ("lf", 1), ("vf", 2), ("vf", 1),
+    ("r", 0), ("l", 0), ("vf", 3), ("vs", 0), ("l", 2), ("dr", 1, 0), ("dr", 1, 2), ("l", 1), ("d", 1, 0, 2),
+    ("d", 1, 2, 2), ("dr", 1, 1), ("d", 1, 1, 2), ("ts", 2), ("d", 1, 0, 1), ("d", 1, 0, 3), ("d", 1, 1, 3),
+    ("d", 1, 2, 1), ("vf", 0), ("re", 1, 0), ("ts", 4), ("ts", 3), ("d", 1, 1, 1), ("ts", 1), ("re", 1, 1),
+    ("d", 1, 2, 3), ("re", 1, 2), ("d", 1, 0, 0), ("d", 1, 2, 0), ("mix", 0), ("d", 1, 1, 0), ("mix", 1), ("tf", 2),
+    ("tf", 4), ("mf", 0), ("tf", 3), ("tf", 1), ("mix", 2), ("mf", 1), ("m", 0), ("dr", 2, 0), ("d", 2, 0, 2),
+    ("d", 2, 0, 3), ("d", 2, 0, 1), ("mf", 2), ("ts", 0), ("m", 1), ("dr", 2, 1), ("d", 2, 1, 2), ("re", 2, 0),
+    ("d", 2, 1, 1), ("d", 2, 1, 3), ("m", 2), ("dr", 2, 2), ("d", 2, 2, 2), ("tf", 0), ("d", 2, 2, 3),
+    ("d", 2, 2, 1), ("re", 2, 1), ("re", 2, 2), ("d", 2, 0, 0), ("d", 2, 1, 0), ("fin", 0), ("d", 2, 2, 0),
+    ("fin", 1), ("fin", 2), ("col", 0), ("col", 1), ("col", 2),
 )
 
 

time: 87.4 us -> 80.7 us (0.923)
  Pallas kernels: 85.2 us -> 78.5 us
    pallas_call x1, Pallas kernels: 85.2 us -> 78.5 us  [per_device(): pl.pallas_call(kernel, out_shape=jax.ShapeDtypeStruct(turned, BF16), in_s...]
where the time goes in v3:
time: 80.7 us; the launch traced here: 80.5 us
  Pallas kernels  78.5 us (97%)
  local copies, waits for them, and re-layouts  2.04 us (3%)
    pallas_call x1, Pallas kernels, per_device(): pl.pallas_call(kernel, out_shape=jax.ShapeDtypeStruct(turned, BF16), in_s...  78.5 us
    unnamed x1, local copies, waits for them, and re-layouts  2.04 us

profile of v3, /device:TPU:1, one launch (start us, length us, event | category | flops | bytes accessed | tf_op | source)
XLA Modules:
  0.0 80.5 jit_solution(16244975662381120682)
XLA Ops:
  0.0 78.5 %cycle.1 = bf16[2,288,576]{2,1,0:T(8,128)(2,1)} custom-call(s32[2]{0:T(128)} %count.1, bf16[2,288,576]{2,1,0:T(8,128)(2,1)} %bitcast.5, bf16[2,288,576]{2,1,0:T(8,128)(2,1)} %bitcast.6, bf16[2,288,576]{2,1,0:T(8,128)(2,1)} %bitcast.7), custom_call_target="tpu_custom_call" | custom-call | flops 6115295232 | bytes 2654208 | tf_op jit(solution)/shard_map/cycle/pallas_call | solution.py:442
  78.5 2.0 %copy.6 = bf16[2,576,288]{1,2,0:T(8,128)(2,1)} copy(bf16[2,576,288]{1,2,0:T(8,128)(2,1)} %bitcast.4) | data formatting | bytes 1327104

commit v4 on v3

--- a/solution.py
+++ b/solution.py
@@ -10,13 +10,19 @@
 MESH = pl.DeviceIdType.MESH
 F32, BF16 = jnp.float32, jnp.bfloat16
 ROWS, COLS = 576, 288
-Q = 3
-R = ROWS // Q
-G = R // 4
-PR = 2 * R + G
+PIECES = (192, 192, 192)
+Q = len(PIECES)
+START = tuple(sum(PIECES[:q]) for q in range(Q))
+RMAX = max(PIECES)
+PMAX = 2 * RMAX + RMAX // 4
 H = ROWS // 2
 RG = 80
 PV = 2 * H + RG
+
+
+def sizes(q):
+    r = PIECES[q]
+    return r, r // 4, 2 * r + r // 4
 
 
 def swap4(parts):
@@ -31,12 +37,12 @@
     return out
 
 SCHEDULE = (
-    ("p", 1), ("b",), ("v", 1), ("p", 0), ("v", 0), ("pt",), ("r", 1), ("vs", 2), ("t", 0), ("vs", 1), ("vs", 4),
-    ("t", 1), ("t", 2), ("lf", 0), ("vs", 3), ("lf", 2), ("vf", 4), ("w",), ("lf", 1), ("vf", 2), ("vf", 1),
-    ("r", 0), ("l", 0), ("vf", 3), ("vs", 0), ("l", 2), ("dr", 1, 0), ("dr", 1, 2), ("l", 1), ("d", 1, 0, 2),
+    ("p", 1), ("b",), ("v", 1), ("p", 0), ("pt",), ("v", 0), ("r", 1), ("r", 0), ("vs", 2), ("t", 0), ("vs", 1),
+    ("vs", 4), ("vs", 3), ("t", 1), ("t", 2), ("lf", 0), ("lf", 2), ("vf", 4), ("w",), ("lf", 1), ("vf", 2),
+    ("vf", 1), ("l", 0), ("vf", 3), ("vs", 0), ("l", 2), ("dr", 1, 0), ("dr", 1, 2), ("l", 1), ("d", 1, 0, 2),
     ("d", 1, 2, 2), ("dr", 1, 1), ("d", 1, 1, 2), ("ts", 2), ("d", 1, 0, 1), ("d", 1, 0, 3), ("d", 1, 1, 3),
-    ("d", 1, 2, 1), ("vf", 0), ("re", 1, 0), ("ts", 4), ("ts", 3), ("d", 1, 1, 1), ("ts", 1), ("re", 1, 1),
-    ("d", 1, 2, 3), ("re", 1, 2), ("d", 1, 0, 0), ("d", 1, 2, 0), ("mix", 0), ("d", 1, 1, 0), ("mix", 1), ("tf", 2),
+    ("d", 1, 2, 1), ("vf", 0), ("re", 1, 0), ("ts", 4), ("d", 1, 1, 1), ("ts", 3), ("d", 1, 2, 3), ("ts", 1),
+    ("re", 1, 1), ("d", 1, 0, 0), ("re", 1, 2), ("mix", 0), ("d", 1, 2, 0), ("d", 1, 1, 0), ("tf", 2), ("mix", 1),
     ("tf", 4), ("mf", 0), ("tf", 3), ("tf", 1), ("mix", 2), ("mf", 1), ("m", 0), ("dr", 2, 0), ("d", 2, 0, 2),
     ("d", 2, 0, 3), ("d", 2, 0, 1), ("mf", 2), ("ts", 0), ("m", 1), ("dr", 2, 1), ("d", 2, 1, 2), ("re", 2, 0),
     ("d", 2, 1, 1), ("d", 2, 1, 3), ("m", 2), ("dr", 2, 2), ("d", 2, 2, 2), ("tf", 0), ("d", 2, 2, 3),
@@ -118,7 +124,8 @@
         dst[h] = jnp.transpose(src[h] * live[h])
 
     def pack_rows(ref, dst, h, q):
-        r0 = q * R
+        R, G, PR = sizes(q)
+        r0 = START[q]
         dst[h, q, 0:R] = ref[h, r0 : r0 + R, 0:128]
         dst[h, q, R : 2 * R] = ref[h, r0 : r0 + R, 128:256]
         strips = [ref[h, r0 + g * G : r0 + g * G + G, 256:288].astype(F32) for g in range(4)]
@@ -199,16 +206,19 @@
     def ring_forward(buf, r1, s2, r2, q):
         for d in (0, 1):
             k, p = at(a, 2 * d - 1), d * Q + q
-            got(buf.at[k, p], r1.at[d, p])
-            send(buf.at[k, p], buf.at[k, p], s2.at[d, q], r2.at[d, q], ring(1 - 2 * d))
+            part = buf.at[k, p, 0 : sizes(q)[2]]
+            got(part, r1.at[d, p])
+            send(part, part, s2.at[d, q], r2.at[d, q], ring(1 - 2 * d))
 
     def ring_last(buf, r1, r2, q):
+        n = sizes(q)[2]
         for d in (0, 1):
             k, p = at(a, 2 * d - 1), (1 - d) * Q + q
-            got(buf.at[k, p], r1.at[d, p])
-            got(buf.at[at(a, 2), d * Q + q], r2.at[d, q])
+            got(buf.at[k, p, 0:n], r1.at[d, p])
+            got(buf.at[at(a, 2), d * Q + q, 0:n], r2.at[d, q])
 
     def make_left(buf, lhs, q):
+        R, G, PR = sizes(q)
         for half in (0, 1):
             p, r0 = half * Q + q, half * R
             for k in range(4):
@@ -218,10 +228,11 @@
                 lhs[q, r0 + g * G : r0 + g * G + G, 1024:1152] = v.astype(BF16)
 
     def dot_rest(st, q):
+        R, G, PR = sizes(q)
         vr = st.ops.r
         y_last(st.ops, 4) if q == 0 else None
         right = jnp.concatenate([vr[k, 0:256] for k in range(4)] + [vr[k, 256:H] for k in range(4)], axis=0)
-        part = jnp.dot(st.lhs[q], right, preferred_element_type=F32)
+        part = jnp.dot(st.lhs[q, 0 : 2 * R], right, preferred_element_type=F32)
         for half in (0, 1):
             p = half * Q + q
             by = swap4([part[half * R + g * G : half * R + g * G + G] for g in range(4)])
@@ -234,11 +245,12 @@
                     st.cs[o - 1, p, 2 * R : PR] = v.astype(BF16)
 
     def dot_main(st, q, o):
+        R, _, PR = sizes(q)
         vm, t = st.ops.m, at(b, o)
         y_last(st.ops, o) if q == 0 else None
         big = [jnp.concatenate([vm[k, t, 0:256], vm[k, t, H : H + 256]], axis=1) for k in range(4)]
         small = [jnp.concatenate([vm[k, t, 256:H], vm[k, t, H + 256 : 2 * H]], axis=1) for k in range(4)]
-        part = jnp.dot(st.lhs[q], jnp.concatenate(big + small, axis=0), preferred_element_type=F32)
+        part = jnp.dot(st.lhs[q, 0 : 2 * R], jnp.concatenate(big + small, axis=0), preferred_element_type=F32)
         for half in (0, 1):
             p = half * Q + q
             for lane in (0, 1):
@@ -249,26 +261,29 @@
                     st.cs[o - 1, p, lane * R : lane * R + R] = v.astype(BF16)
         if o == 2:
             for d in (0, 1):
-                send(st.cs.at[1, d * Q + q], st.l1.at[d, q], st.s1.at[d, q], st.r1.at[d, q], line(1 - 2 * d))
+                send(st.cs.at[1, d * Q + q, 0:PR], st.l1.at[d, q, 0:PR], st.s1.at[d, q], st.r1.at[d, q], line(1 - 2 * d))
         elif o:
             d = o // 2
             p = (1 - d) * Q + q
-            send(st.cs.at[2 * d, p], st.l2.at[d, p], st.s2.at[d, p], st.r2.at[d, p], line(1 - 2 * d))
+            send(st.cs.at[2 * d, p, 0:PR], st.l2.at[d, p, 0:PR], st.s2.at[d, p], st.r2.at[d, p], line(1 - 2 * d))
 
     def relay(st, q):
+        PR = sizes(q)[2]
         for d in (0, 1):
             p = d * Q + q
-            got(st.l1.at[d, q], st.r1.at[d, q])
-            st.cs[2 * d, p] = (st.cs[2 * d, p].astype(F32) + st.l1[d, q].astype(F32)).astype(BF16)
-            send(st.cs.at[2 * d, p], st.l2.at[d, p], st.s2.at[d, p], st.r2.at[d, p], line(1 - 2 * d))
-
-    def total(st, p):
-        for d in (0, 1):
-            got(st.l2.at[d, p], st.r2.at[d, p])
-        return st.own[p] + st.l2[0, p].astype(F32) + st.l2[1, p].astype(F32)
+            got(st.l1.at[d, q, 0:PR], st.r1.at[d, q])
+            st.cs[2 * d, p, 0:PR] = (st.cs[2 * d, p, 0:PR].astype(F32) + st.l1[d, q, 0:PR].astype(F32)).astype(BF16)
+            send(st.cs.at[2 * d, p, 0:PR], st.l2.at[d, p, 0:PR], st.s2.at[d, p], st.r2.at[d, p], line(1 - 2 * d))
+
+    def total(st, half, q):
+        p, n = half * Q + q, sizes(q)[2]
+        for d in (0, 1):
+            got(st.l2.at[d, p, 0:n], st.r2.at[d, p])
+        return st.own[p, 0:n] + st.l2[0, p, 0:n].astype(F32) + st.l2[1, p, 0:n].astype(F32)
 
     def unpack(v, h, q):
-        r0 = q * R
+        R, G, PR = sizes(q)
+        r0 = START[q]
         o_t[h, r0 : r0 + R, 0:128] = v[0:R].astype(BF16)
         o_t[h, r0 : r0 + R, 128:256] = v[R : 2 * R].astype(BF16)
         for g in range(4):
@@ -278,10 +293,10 @@
             o_t[h, r0 + g * G : r0 + g * G + G, 256:288] = strip[:, 0:32].astype(BF16)
 
     def turn_back(h, q):
-        if q == 1:
-            out[h, :, 0:384] = jnp.transpose(o_t[h, 0:384])
-        if q == 2:
-            out[h, :, 384:576] = jnp.transpose(o_t[h, 384:576])
+        if q == Q - 2:
+            out[h, :, 0 : START[Q - 1]] = jnp.transpose(o_t[h, 0 : START[Q - 1]])
+        if q == Q - 1:
+            out[h, :, START[Q - 1] : ROWS] = jnp.transpose(o_t[h, START[Q - 1] : ROWS])
 
     v_ops = Ops(vp, vm, vr, vx, v_as, v_ar, v_s1, v_r1, v_s2, v_r2)
     t_ops = Ops(tp, tm, tr, tx, t_as, t_ar, t_s1, t_r1, t_s2, t_r2)
@@ -310,15 +325,17 @@
             for q in range(Q):
                 pack_rows(t_t, ts, h, q)
         for q in range(Q):
-            tl[a, c * Q + q] = ts[c, q]
+            n = sizes(q)[2]
+            tl[a, c * Q + q, 0:n] = ts[c, q, 0:n]
 
     def step_t(q):
+        n = sizes(q)[2]
         for h in range(2):
             for d in (0, 1):
                 to = dev(dz=1 - 2 * d, core=0) if h == 0 else dev(dx=1 - 2 * d, core=1)
-                place = z if h == 0 else x
-                send(ts.at[h, q], tl.at[place, c * Q + q], tl_s1.at[d, h, q], tl_r1.at[d, c * Q + q], to)
-        send(ts.at[1 - c, q], tl.at[b, c * Q + q], tl_sw.at[0, q], tl_sw.at[1, q], partner)
+                dst = tl.at[z if h == 0 else x, c * Q + q, 0:n]
+                send(ts.at[h, q, 0:n], dst, tl_s1.at[d, h, q], tl_r1.at[d, c * Q + q], to)
+        send(ts.at[1 - c, q, 0:n], tl.at[b, c * Q + q, 0:n], tl_sw.at[0, q], tl_sw.at[1, q], partner)
 
     def step_r(h):
         for s in range(2):
@@ -331,38 +348,42 @@
             turn(w_in, w_t, h)
             for q in range(Q):
                 pack_rows(w_t, ws, h, q)
-        send(ws.at[1 - c], wp.at[pl.ds(c * Q, Q)], w_sw.at[0], w_sw.at[1], partner)
         for q in range(Q):
-            wp[c * Q + q] = ws[c, q]
+            n = sizes(q)[2]
+            send(ws.at[1 - c, q, 0:n], wp.at[c * Q + q, 0:n], w_sw.at[0, q], w_sw.at[1, q], partner)
+            wp[c * Q + q, 0:n] = ws[c, q, 0:n]
 
     def step_left(q):
         ring_last(tl, tl_r1, tl_r2, q)
-        got(tl.at[a, (1 - c) * Q + q], tl_sw.at[1, q])
+        got(tl.at[a, (1 - c) * Q + q, 0 : sizes(q)[2]], tl_sw.at[1, q])
         make_left(tl, lhs1, q)
 
     def step_mix(q):
-        if q == 0:
-            got(wp.at[pl.ds((1 - c) * Q, Q)], w_sw.at[1])
+        n = sizes(q)[2]
+        got(wp.at[(1 - c) * Q + q, 0:n], w_sw.at[1, q])
         for half in (0, 1):
             p = half * Q + q
-            mb[a, p] = (wp[p].astype(F32) + 0.5 * total(stages[1], p)).astype(BF16)
+            mb[a, p, 0:n] = (wp[p, 0:n].astype(F32) + 0.5 * total(stages[1], half, q)).astype(BF16)
+            part = mb.at[a, p, 0:n]
             for d in (0, 1):
-                send(mb.at[a, p], mb.at[a, p], m_s1.at[d, p], m_r1.at[d, p], ring(1 - 2 * d))
+                send(part, part, m_s1.at[d, p], m_r1.at[d, p], ring(1 - 2 * d))
 
     def step_mixed(q):
         ring_last(mb, m_r1, m_r2, q)
         make_left(mb, lhs2, q)
 
     def step_finish(q):
+        n = sizes(q)[2]
         for half in (0, 1):
-            fo[half, q] = total(stages[2], half * Q + q).astype(BF16)
-        send(fo.at[1 - c, q], ob.at[q], o_s.at[q], o_r.at[q], partner)
-        unpack(fo[c, q].astype(F32), c, q)
+            fo[half, q, 0:n] = total(stages[2], half, q).astype(BF16)
+        send(fo.at[1 - c, q, 0:n], ob.at[q, 0:n], o_s.at[q], o_r.at[q], partner)
+        unpack(fo[c, q, 0:n].astype(F32), c, q)
         turn_back(c, q)
 
     def step_collect(q):
-        got(ob.at[q], o_r.at[q])
-        unpack(ob[q].astype(F32), 1 - c, q)
+        n = sizes(q)[2]
+        got(ob.at[q, 0:n], o_r.at[q])
+        unpack(ob[q, 0:n].astype(F32), 1 - c, q)
         turn_back(1 - c, q)
 
     steps = {
@@ -417,7 +438,7 @@
     turned, shard = (2, COLS, ROWS), (2, ROWS, COLS)
 
     def piece(*lead, dtype=BF16):
-        return pltpu.VMEM((*lead, PR, 128), dtype)
+        return pltpu.VMEM((*lead, PMAX, 128), dtype)
 
     def right():
         return [
@@ -428,13 +449,13 @@
 
     def sums():
         return [
-            pltpu.VMEM((Q, 2 * R, 1152), BF16), piece(3, 2 * Q), piece(2 * Q, dtype=F32), piece(2, Q), piece(2, 2 * Q),
+            pltpu.VMEM((Q, 2 * RMAX, 1152), BF16), piece(3, 2 * Q), piece(2 * Q, dtype=F32), piece(2, Q), piece(2, 2 * Q),
             dma((2, Q)), dma((2, Q)), dma((2, 2 * Q)), dma((2, 2 * Q)),
         ]
 
     scratch = [pltpu.VMEM(turned, BF16)] * 3 + [dma((3,)), pltpu.VMEM(turned, BF16)] + [pltpu.VMEM(shard, BF16)] * 3
     scratch += [piece(2, Q), piece(4, 2 * Q), dma((2, 2, Q)), dma((2, 2 * Q)), dma((2, Q)), dma((2, Q)), dma((2, Q))]
-    scratch += [piece(2, Q), piece(2 * Q), dma((2,))]
+    scratch += [piece(2, Q), piece(2 * Q), dma((2, Q))]
     scratch += right() + right()
     scratch += [piece(4, 2 * Q), dma((2, 2 * Q)), dma((2, 2 * Q)), dma((2, Q)), dma((2, Q))]
     scratch += sums() + sums()

time: 80.7 us -> 79 us (0.979)
  Pallas kernels: 78.5 us -> 76.8 us
    pallas_call x1, Pallas kernels: 78.5 us -> 76.8 us  [per_device(): pl.pallas_call(kernel, out_shape=jax.ShapeDtypeStruct(turned, BF16), in_s...]
where the time goes in v4:
time: 79 us; the launch traced here: 78.8 us
  Pallas kernels  76.8 us (97%)
  local copies, waits for them, and re-layouts  2.04 us (3%)
    pallas_call x1, Pallas kernels, per_device(): pl.pallas_call(kernel, out_shape=jax.ShapeDtypeStruct(turned, BF16), in_s...  76.8 us
    unnamed x1, local copies, waits for them, and re-layouts  2.04 us

profile of v4, /device:TPU:1, one launch (start us, length us, event | category | flops | bytes accessed | tf_op | source)
XLA Modules:
  0.0 78.8 jit_solution(15987842774227938274)
XLA Ops:
  0.0 76.8 %cycle.1 = bf16[2,288,576]{2,1,0:T(8,128)(2,1)} custom-call(s32[2]{0:T(128)} %count.1, bf16[2,288,576]{2,1,0:T(8,128)(2,1)} %bitcast.5, bf16[2,288,576]{2,1,0:T(8,128)(2,1)} %bitcast.6, bf16[2,288,576]{2,1,0:T(8,128)(2,1)} %bitcast.7), custom_call_target="tpu_custom_call" | custom-call | flops 6115295232 | bytes 2654208 | tf_op jit(solution)/shard_map/cycle/pallas_call | solution.py:463
  76.8 2.0 %copy.6 = bf16[2,576,288]{1,2,0:T(8,128)(2,1)} copy(bf16[2,576,288]{1,2,0:T(8,128)(2,1)} %bitcast.4) | data formatting | bytes 1327104
